TPU v7x, 32 devices: a whole 2x2x4 slice. The times are simulated.
32 devices in a mesh: ctx: 4 (over y, core), head: 2 (over x), rep: 4 (over z).
Axes of the slice: x: 2, y: 2, z: 4, core: 2. Of those that a mesh axis runs over, the one named last changes fastest.
Arguments:
- q_turn: bfloat16 [1024, 8192], P(('rep', 'ctx', 'head')), parts along dimension 0, may hold values from -18 to 18
- k_turn: bfloat16 [1024, 1024], P(('rep', 'ctx', 'head')), parts along dimension 0, may hold values from -6 to 6
- v_turn: bfloat16 [1024, 1024], P(('rep', 'ctx', 'head')), parts along dimension 0, may hold values from -6 to 6
- cache_k: bfloat16 [512, 64, 1024], P(('rep', 'ctx'), None, 'head'), parts along dimension 0, may hold values from -6 to 6
- cache_v: bfloat16 [512, 64, 1024], P(('rep', 'ctx'), None, 'head'), parts along dimension 0, may hold values from -6 to 6
- k_scale: float32 [512, 8], P(('rep', 'ctx'), 'head'), parts along dimension 0, may hold values from 0.25 to 2
- v_scale: float32 [512, 8], P(('rep', 'ctx'), 'head'), parts along dimension 0, may hold values from 0.25 to 2
- page_map: int32 [512], P(('rep', 'ctx')), parts along dimension 0, may hold values from 0 to 127, as said below
Outputs:
- attn_out: bfloat16 [1024, 8192], P(('rep', 'ctx'), 'head'), parts along dimension 0
- cache_k_paired: bfloat16 [32768, 1024], P(('rep', 'ctx'), 'head'), parts along dimension 0
- cache_v_paired: bfloat16 [32768, 1024], P(('rep', 'ctx'), 'head'), parts along dimension 0
There are 4 independent parts, one for each index of `rep`. A program takes and returns all parts, laid end to end along the dimension named above; each array names one. Nothing has to cross between parts.
Inputs may be any that keep to these rules, and one draw needn't show every extreme that they name: A permutation: slot s holds logical page page_map[s]. Cut the 128 logical pages into 8 blocks of 16 consecutive pages; the 32 slots of each index of ctx hold exactly one page of every block.
All inputs are finite; a program needn't handle non-finite values.
Results may differ from a plain program's by a relative error of at most 0.0087.
Values may be sent and summed in bfloat16 or wider, within the bound.
A program may use at most 128 MiB of HBM per device.

v0:
```python
import math

import jax
import jax.numpy as jnp
from jax import lax
from jax.sharding import PartitionSpec as P


def joined(value, axis, join):
    pieces = jax.tree.map(lambda part: lax.all_gather(part, axis), value)
    head = jax.tree.map(lambda part: part[0], pieces)
    tail = jax.tree.map(lambda part: part[1:], pieces)
    so_far, _ = lax.scan(lambda so_far, share: (join(so_far, share), None), head, tail)
    return so_far


def scale_pages(codes, scales):
    slots, page_rows, width = codes.shape
    heads = scales.shape[1]
    full = (
        codes.astype(jnp.float32).reshape(slots, page_rows, heads, width // heads)
        * scales[:, None, :, None]
    )
    return full.reshape(slots, page_rows, width).astype(jnp.bfloat16)


def attend(queries, keys, values, turn_keys, turn_values, key_start, head_dim):
    length = queries.shape[0]
    q_heads = queries.shape[1] // head_dim
    kv_heads = keys.shape[1] // head_dim
    per_group = q_heads // kv_heads
    factor = 1.0 / math.sqrt(head_dim)
    by_head = queries.reshape(length, q_heads, head_dim).transpose(1, 0, 2)
    cache_kh = keys.reshape(keys.shape[0], kv_heads, head_dim)
    cache_vh = values.reshape(values.shape[0], kv_heads, head_dim)
    turn_kh = turn_keys.reshape(turn_keys.shape[0], kv_heads, head_dim)
    turn_vh = turn_values.reshape(turn_values.shape[0], kv_heads, head_dim)
    places = key_start + jnp.arange(turn_keys.shape[0], dtype=jnp.int32)
    visible = places[None, :] <= jnp.arange(length, dtype=jnp.int32)[:, None]
    dims = (((1,), (1,)), ((), ()))

    def one_head(pair):
        query, index = pair
        kv_index = index // per_group
        ck = lax.dynamic_index_in_dim(cache_kh, kv_index, 1, keepdims=False)
        cv = lax.dynamic_index_in_dim(cache_vh, kv_index, 1, keepdims=False)
        tk = lax.dynamic_index_in_dim(turn_kh, kv_index, 1, keepdims=False)
        tv = lax.dynamic_index_in_dim(turn_vh, kv_index, 1, keepdims=False)
        cached = lax.dot_general(query, ck, dims, preferred_element_type=jnp.float32) * factor
        recent = lax.dot_general(query, tk, dims, preferred_element_type=jnp.float32) * factor
        recent = jnp.where(visible, recent, -jnp.inf)
        peak = jnp.maximum(jnp.max(cached, axis=1), jnp.max(recent, axis=1))
        cached_e = jnp.exp(cached - peak[:, None])
        recent_e = jnp.exp(recent - peak[:, None])
        total = jnp.sum(cached_e, axis=1) + jnp.sum(recent_e, axis=1)
        mixed = jnp.dot(cached_e.astype(jnp.bfloat16), cv, preferred_element_type=jnp.float32)
        mixed = mixed + jnp.dot(
            recent_e.astype(jnp.bfloat16), tv, preferred_element_type=jnp.float32
        )
        return (mixed, peak, total)

    mixed, peak, total = lax.map(one_head, (by_head, jnp.arange(q_heads, dtype=jnp.int32)))
    return (mixed.transpose(1, 0, 2), peak.T, total.T)


def combine_parts(first, second):
    peak_a, total_a, mixed_a = first
    peak_b, total_b, mixed_b = second
    peak = jnp.maximum(peak_a, peak_b)
    weight_a = jnp.exp(peak_a - peak)
    weight_b = jnp.exp(peak_b - peak)
    total = total_a * weight_a + total_b * weight_b
    mixed = mixed_a * weight_a[..., None] + mixed_b * weight_b[..., None]
    return (peak, total, mixed)


def local(q_turn, k_turn, v_turn, cache_k, cache_v, k_scale, v_scale, page_map):
    ctx_count = lax.axis_size("ctx")
    position = lax.axis_index("ctx")
    slots, page_rows, width = cache_k.shape
    head_dim = width // k_scale.shape[1]
    half = slots // 2
    total_pages = slots * ctx_count
    per_peer = slots // ctx_count
    q_mine, k_mine, v_mine = (
        lax.all_to_all(q_turn, "head", split_axis=1, concat_axis=0, tiled=True),
        lax.all_to_all(k_turn, "head", split_axis=1, concat_axis=0, tiled=True),
        lax.all_to_all(v_turn, "head", split_axis=1, concat_axis=0, tiled=True),
    )
    queries = lax.all_gather(q_mine, "ctx", axis=0, tiled=True)
    own_rows = k_mine.shape[0]
    key_start = position * own_rows
    scaled_k = scale_pages(cache_k, k_scale)
    scaled_v = scale_pages(cache_v, v_scale)

    def owner_of(pages):
        block = pages // half
        return jnp.where(block < ctx_count, block, 2 * ctx_count - 1 - block)

    order = jnp.argsort(owner_of(page_map) * total_pages + page_map)
    send_k = scaled_k[order].reshape(slots * page_rows, width)
    send_v = scaled_v[order].reshape(slots * page_rows, width)
    every_map = lax.all_gather(page_map, "ctx", axis=0, tiled=True)
    recv_k, recv_v = (
        lax.all_to_all(send_k, "ctx", split_axis=0, concat_axis=0, tiled=True),
        lax.all_to_all(send_v, "ctx", split_axis=0, concat_axis=0, tiled=True),
    )
    maps = every_map.reshape(ctx_count, slots)
    mine = owner_of(maps) == position
    ranked = jnp.sort(jnp.where(mine, maps, maps + total_pages), axis=1)[:, :per_peer]
    arrived = ranked.reshape(slots)
    within = arrived % half
    place = jnp.where(arrived // half == position, within, half + within)
    back = jnp.argsort(place)
    paired_k = recv_k.reshape(slots, page_rows, width)[back].reshape(slots * page_rows, width)
    paired_v = recv_v.reshape(slots, page_rows, width)[back].reshape(slots * page_rows, width)
    mixed, peak, total = attend(
        queries,
        scaled_k.reshape(slots * page_rows, width),
        scaled_v.reshape(slots * page_rows, width),
        k_mine,
        v_mine,
        key_start,
        head_dim,
    )
    peak_all, total_all, mixed_all = joined((peak, total, mixed), "ctx", combine_parts)
    mixed_own = lax.dynamic_slice_in_dim(mixed_all, key_start, own_rows, 0)
    total_own = lax.dynamic_slice_in_dim(total_all, key_start, own_rows, 0)
    attn_out = (mixed_own / total_own[..., None]).reshape(own_rows, -1).astype(jnp.bfloat16)
    return (attn_out, paired_k, paired_v)


def solution(mesh):
    return jax.shard_map(
        local,
        mesh=mesh,
        in_specs=(
            P(("rep", "ctx", "head"), None),
            P(("rep", "ctx", "head"), None),
            P(("rep", "ctx", "head"), None),
            P(("rep", "ctx"), None, "head"),
            P(("rep", "ctx"), None, "head"),
            P(("rep", "ctx"), "head"),
            P(("rep", "ctx"), "head"),
            P(("rep", "ctx")),
        ),
        out_specs=(P(("rep", "ctx"), "head"), P(("rep", "ctx"), "head"), P(("rep", "ctx"), "head")),
        check_vma=False,
    )
```

profile of v0, /device:TPU:0, one launch (start us, length us, event | category | flops | bytes accessed | tf_op | source)
XLA Modules:
  0.0 546.2 jit_solution(3927595879535294170)
XLA Ops:
  8.5 12.6 %all_to_all.69 = bf16[32,2,4096]{2,0,1:T(8,128)(2,1)} all-to-all(bf16[32,2,4096]{2,0,1:T(8,128)(2,1)S(1)} %bitcast.132), channel_id=1, replica_groups=mesh['ctx'=4,'head'=2,'rep'=4] {'head'}, dimensions={1} | all-to-all | bytes 1048576 | tf_op jit(solution)/shard_map/all_to_all | solution.py:86
  21.7 3.3 all-to-all-start.1
  29.1 3.3 all-to-all-start.2
  32.5 4.0 reshape_reshape.6
  36.5 3.2 copy.69
  41.7 3.2 copy.71
  45.0 4.1 copy.63
  49.1 281.5 %while.32 = (s32[]{:T(128)}, f32[32,256,128]{2,1,0:T(8,128)}, f32[32,256]{1,0:T(8,128)S(1)}, f32[32,256]{1,0:T(8,128)S(1)}, bf16[32,256,128]{1,2,0:T(8,128)(2,1)...) while((s32[]{:T(128)}, f32[32,256,128]{2,1,0:T(8,128)}, ...), condition=%wide.region_5.6_spmd.clone, body=%wide.region_0.5_spmd.clone.sunk | while | flops 280133120 | bytes 8114553 | solution.py:62
  64.5 2.2 fusion.63
  73.3 2.2 fusion.63
  90.9 2.2 fusion.63
  117.3 2.2 fusion.63
  134.9 2.2 fusion.63
  258.0 2.2 fusion.63
  332.8 5.2 all-reduce
  342.8 4.8 all-to-all-start.3
  349.6 46.5 %all-to-all-done.3 = bf16[4,512,512]{2,1,0:T(8,128)(2,1)} async-done(((bf16[4,512,512]{2,1,0:T(8,128)(2,1)}), bf16[4,512,512]{2,1,0:T(8,128)(2,1)}, u32[]{:S(2)}, u32[]{:S(2)}) %all-to-all-start.3) | async-done | bytes 2097184 | tf_op jit(solution)/shard_map/all_to_all | solution.py:105
  396.2 3.6 all-to-all-start.4
  401.4 3.6 gather_fusion.1
  405.0 43.2 %all-to-all-done.4 = bf16[4,512,512]{2,1,0:T(8,128)(2,1)S(1)} async-done(((bf16[4,512,512]{2,1,0:T(8,128)(2,1)}), bf16[4,512,512]{2,1,0:T(8,128)(2,1)S(1)}, u32[]{:S(2)}, u32[]{:S(2)}) %all-to-all-start.4) | async-done | bytes 2097184 | tf_op jit(solution)/shard_map/all_to_all | solution.py:106
  450.2 6.1 %all-gather = f32[1024,32]{0,1:T(8,128)S(1)} all-gather(f32[256,32]{0,1:T(8,128)S(1)} %bitcast.146), channel_id=2, replica_groups=mesh['ctx'=4,'head'=2,'rep'=4] {'ctx'}, dimensions={0}, use_global_device_ids=true | all-gather | bytes 163840 | tf_op jit(solution)/shard_map/all_gather | solution.py:10
  456.3 6.4 %all-gather.1 = f32[1024,32]{0,1:T(8,128)S(1)} all-gather(f32[256,32]{0,1:T(8,128)S(1)} %bitcast.145), channel_id=3, replica_groups=mesh['ctx'=4,'head'=2,'rep'=4] {'ctx'}, dimensions={0}, use_global_device_ids=true | all-gather | bytes 163840 | tf_op jit(solution)/shard_map/all_gather | solution.py:10
  463.3 21.8 %all-gather.8.cloned.1.call-done = f32[1024,32,128]{2,0,1:T(8,128)} async-done(((f32[256,32,128]{2,0,1:T(8,128)}), f32[1024,32,128]{2,0,1:T(8,128)}) %all-gather.8.cloned.1.call-update) | async-done | bytes 16777232 | tf_op jit(solution)/shard_map/all_gather | solution.py:10
  487.3 4.4 copy.75
  491.6 10.5 %slice.47 = f32[768,32,128]{2,0,1:T(8,128)} slice(f32[1024,32,128]{2,0,1:T(8,128)} %all-gather.8.cloned.1.call-done), slice={[256:1024], [0:32], [0:128]} | slice | bytes 25165824 | tf_op jit(solution)/shard_map/slice | solution.py:12
  502.2 34.6 %while.31 = (s32[]{:T(128)}, f32[256,32]{1,0:T(8,128)S(1)}, f32[256,32]{1,0:T(8,128)S(1)}, f32[256,32,128]{2,1,0:T(8,128)}, f32[3,256,32]{2,1,0:T(8,128)S(1)}, /...) while((s32[]{:T(128)}, f32[256,32]{1,0:T(8,128)S(1)}, f32[256,32]{1,0:T(8,128)S(1)}, ...), condition=%wide.region_7.8_spmd, body=%wide.region_6.7_spmd.sunk | while | flops 3194882 | bytes 54853780 | solution.py:13
  502.3 2.6 constant_dynamic-slice_fusion.3
  505.7 6.0 %fusion.55 = f32[256,32,128]{2,1,0:T(8,128)S(1)} fusion(f32[1,256,32,128]{3,1,0,2:T(8,128)S(1)} %constant_dynamic-slice_fusion.3, f32[256,32,128]{2,1,0:T(8,128)S(1)} %copy-done, f32[256,32]{1,0:T(8,128)S(1)} %get-tuple-element.434, f32[256,32]{1,0:T(8,128)S(1)} %get-tuple-element.435), kind=kLoop, calls=%fused_computation.7.clone.1 | loop fusion | flops 3145728 | bytes 12648448 | tf_op jit(solution)/shard_map/while/body/eval_jaxpr/add | solution.py:73
  513.8 2.6 constant_dynamic-slice_fusion.3
  517.3 6.0 %fusion.55 = f32[256,32,128]{2,1,0:T(8,128)S(1)} fusion(f32[1,256,32,128]{3,1,0,2:T(8,128)S(1)} %constant_dynamic-slice_fusion.3, f32[256,32,128]{2,1,0:T(8,128)S(1)} %copy-done, f32[256,32]{1,0:T(8,128)S(1)} %get-tuple-element.434, f32[256,32]{1,0:T(8,128)S(1)} %get-tuple-element.435), kind=kLoop, calls=%fused_computation.7.clone.1 | loop fusion | flops 3145728 | bytes 12648448 | tf_op jit(solution)/shard_map/while/body/eval_jaxpr/add | solution.py:73
  525.4 2.6 constant_dynamic-slice_fusion.3
  528.8 6.0 %fusion.55 = f32[256,32,128]{2,1,0:T(8,128)S(1)} fusion(f32[1,256,32,128]{3,1,0,2:T(8,128)S(1)} %constant_dynamic-slice_fusion.3, f32[256,32,128]{2,1,0:T(8,128)S(1)} %copy-done, f32[256,32]{1,0:T(8,128)S(1)} %get-tuple-element.434, f32[256,32]{1,0:T(8,128)S(1)} %get-tuple-element.435), kind=kLoop, calls=%fused_computation.7.clone.1 | loop fusion | flops 3145728 | bytes 12648448 | tf_op jit(solution)/shard_map/while/body/eval_jaxpr/add | solution.py:73
  (447 shorter events, 218.5 us)
Async XLA Ops:
  7.2 13.9 %copy-start.7 = (bf16[32,1024]{1,0:T(8,128)(2,1)S(1)}, bf16[32,1024]{1,0:T(8,128)(2,1)}, u32[]{:S(2)}) copy-start(bf16[32,1024]{1,0:T(8,128)(2,1)} %param.13) | copy-start | bytes 196612
  7.2 17.9 %copy-start.9 = (f32[32,4]{0,1:T(4,128)S(1)}, f32[32,4]{0,1:T(4,128)}, u32[]{:S(2)}) copy-start(f32[32,4]{0,1:T(4,128)} %param.17) | copy-start | bytes 1540
  7.2 18.1 %copy-start.10 = (f32[32,4]{0,1:T(4,128)S(1)}, f32[32,4]{0,1:T(4,128)}, u32[]{:S(2)}) copy-start(f32[32,4]{0,1:T(4,128)} %param.18) | copy-start | bytes 1540
  7.2 18.3 %copy-start.5 = (bf16[32,64,512]{2,1,0:T(8,128)(2,1)S(1)}, bf16[32,64,512]{2,1,0:T(8,128)(2,1)}, u32[]{:S(2)}) copy-start(bf16[32,64,512]{2,1,0:T(8,128)(2,1)} %param.15) | copy-start | bytes 6291460
  7.2 37.8 %all-gather.6.cloned.1.call-start = ((), (), s32[]{:S(2)}) async-start(), calls=%async_computation.5 | async-start | bytes 2621440 | tf_op jit(solution)/shard_map/all_gather | solution.py:90
  21.7 7.4 %all-to-all-start.1 = ((bf16[32,2,512]{2,0,1:T(8,128)(2,1)}), bf16[32,2,512]{2,0,1:T(8,128)(2,1)S(1)}, u32[]{:S(2)}, u32[]{:S(2)}) async-start(bf16[32,2,512]{2,0,1:T(8,128)(2,1)} %bitcast.95), calls=%async_computation.1 | async-start | bytes 131072 | tf_op jit(solution)/shard_map/all_to_all | solution.py:87
  25.5 1.9 copy-start.6
  27.4 0.8 copy-start.8
  27.9 11.8 %copy-start.2 = (bf16[32,64,512]{2,1,0:T(8,128)(2,1)}, bf16[32,64,512]{2,1,0:T(8,128)(2,1)S(1)}, u32[]{:S(2)}) copy-start(bf16[32,64,512]{2,1,0:T(8,128)(2,1)S(1)} %multiply_convert_fusion) | copy-start | bytes 6291460
  29.1 15.8 %all-to-all-start.2 = ((bf16[32,2,512]{2,0,1:T(8,128)(2,1)}), bf16[32,2,512]{2,0,1:T(8,128)(2,1)S(1)}, u32[]{:S(2)}, u32[]{:S(2)}) async-start(bf16[32,2,512]{2,0,1:T(8,128)(2,1)} %bitcast.94), calls=%async_computation.2 | async-start | bytes 131072 | tf_op jit(solution)/shard_map/all_to_all | solution.py:88
  32.5 452.6 %all-gather.8.cloned.1.call-start = ((), (), s32[]{:S(2)}) async-start(), calls=%async_computation.6 | async-start | bytes 20971520 | tf_op jit(solution)/shard_map/all_gather | solution.py:10
  330.6 0.7 copy-start.12
  330.6 1.9 copy-start.11
  330.6 10.2 %copy-start.4 = (bf16[32,64,512]{2,1,0:T(8,128)(2,1)S(1)}, bf16[32,64,512]{2,1,0:T(8,128)(2,1)}, u32[]{:S(2)}) copy-start(bf16[32,64,512]{2,1,0:T(8,128)(2,1)} %multiply_convert_fusion.1) | copy-start | bytes 6291460
  342.8 4.8 copy-start.3
  342.8 53.3 %all-to-all-start.3 = ((bf16[4,512,512]{2,1,0:T(8,128)(2,1)}), bf16[4,512,512]{2,1,0:T(8,128)(2,1)}, u32[]{:S(2)}, u32[]{:S(2)}) async-start(bf16[4,512,512]{2,1,0:T(8,128)(2,1)} %bitcast.123), calls=%async_computation.3 | async-start | bytes 4194304 | tf_op jit(solution)/shard_map/all_to_all | solution.py:105
  396.2 52.1 %all-to-all-start.4 = ((bf16[4,512,512]{2,1,0:T(8,128)(2,1)}), bf16[4,512,512]{2,1,0:T(8,128)(2,1)S(1)}, u32[]{:S(2)}, u32[]{:S(2)}) async-start(bf16[4,512,512]{2,1,0:T(8,128)(2,1)} %bitcast.121), calls=%async_computation.4 | async-start | bytes 4194304 | tf_op jit(solution)/shard_map/all_to_all | solution.py:106
  485.1 2.2 slice-start
  502.3 3.5 copy-start
  511.7 1.9 copy-start.1
  513.8 3.5 copy-start
  523.3 1.9 copy-start.1
  525.3 3.5 copy-start
  534.8 1.9 copy-start.1
Sparse Core Ops, SparseCore 0:
  21.2 23.1 all-gather.5
  330.8 154.2 all-gather.7
where the time goes:
time: 552 us; the launch traced here: 546 us
  matrix products  161 us (29%)
  waiting for transfers between devices  112 us (20%)
  local copies, waits for them, and re-layouts  87.9 us (16%)
  loops' own time  83.7 us (15%)
  other arithmetic  41.8 us (8%)
  blocking collectives  30.3 us (5%)
  starting transfers between devices  15.1 us (3%)
  between operations  15.1 us (3%)
    another operation x1, loops' own time, attend(): lax.map(one_head, (by_head, jnp.arange(q_heads, dtype=jnp.int32)))  83.6 us
    dot_general x32, matrix products, one_head(): jnp.dot(cached_e.astype(jnp.bfloat16), cv, preferred_element_type=jnp.flo...  70.2 us
    dot_general x32, matrix products, one_head(): lax.dot_general(query, ck, dims, preferred_element_type=jnp.float32)  52 us
    all_to_all x1, waiting for transfers between devices, local(): lax.all_to_all(send_k, 'ctx', split_axis=0, concat_axis=0, tiled=True)  46.5 us
    all_to_all x1, waiting for transfers between devices, local(): lax.all_to_all(send_v, 'ctx', split_axis=0, concat_axis=0, tiled=True)  43.2 us
    dot_general x32, matrix products, one_head(): lax.dot_general(query, tk, dims, preferred_element_type=jnp.float32)  32 us
    all_gather x1, waiting for transfers between devices, joined(): pieces = jax.tree.map(lambda part: lax.all_gather(part, axis), value)  21.8 us
    dynamic_slice x32, local copies, waits for them, and re-layouts, attend(): lax.map(one_head, (by_head, jnp.arange(q_heads, dtype=jnp.int32)))  19.7 us
  transfers between devices with their start and end apart: 6, of which 4 were waited for; matrix products, arithmetic and copies ran while one was open for 6% of the time, Pallas kernels for 0%

commit v1 on v0

v1 whole, which is shorter than its diff:
```python
import functools
import math

import jax
import jax.numpy as jnp
from jax import lax
from jax.experimental import pallas as pl
from jax.experimental.pallas import tpu as pltpu
from jax.sharding import PartitionSpec as P

MESH = pl.DeviceIdType.MESH
NT = (((1,), (1,)), ((), ()))


def main_kernel(
    n,
    heads,
    head_dim,
    order,
    k_scale,
    v_scale,
    page_map,
    q_turn,
    k_turn,
    v_turn,
    cache_k,
    cache_v,
    out,
    recv_k,
    recv_v,
    maps,
    raw_k,
    raw_v,
    sent_k,
    sent_v,
    q_all,
    k_mine,
    v_mine,
    acc,
    stats,
    sib_acc,
    sib_stats,
    far_out,
    far_out_stats,
    far_in,
    far_in_stats,
    local_sem,
    swap_send,
    swap_recv,
    far_q_send,
    far_q_recv,
    near_q_send,
    near_q_recv,
    page_send,
    page_recv,
    map_send,
    map_recv,
    near_send,
    near_recv,
    far_send,
    far_recv,
):
    c = lax.axis_index("ctx")
    h = lax.axis_index("head")
    chips = n // 2
    chip, core = c // 2, c % 2
    sibling = chip * 2 + (1 - core)
    slots, page_rows, width = raw_k.shape
    per_peer = slots // n
    part_rows, q_width = q_all.shape[2], q_all.shape[3]
    rows = heads * part_rows
    kv_heads = width // head_dim
    q_heads = q_width // head_dim
    per_group = q_heads // kv_heads
    factor = 1.0 / math.sqrt(head_dim)

    def remote(src, dst, send, recv, **where):
        return pltpu.make_async_remote_copy(
            src_ref=src,
            dst_ref=dst,
            send_sem=send,
            recv_sem=recv,
            device_id=where,
            device_id_type=MESH,
        )

    def same_core(d):
        return lax.rem(chip + d, chips) * 2 + core

    def other_core(d):
        return lax.rem(chip + d, chips) * 2 + (1 - core)

    pages_in = [
        pltpu.make_async_copy(cache_k, raw_k, local_sem.at[0]),
        pltpu.make_async_copy(cache_v, raw_v, local_sem.at[1]),
    ]
    for copy in pages_in:
        copy.start()
    own_turn = [
        pltpu.make_async_copy(
            src.at[:, pl.ds(pl.multiple_of(h * size, size), size)], dst, local_sem.at[2 + i]
        )
        for i, (src, dst, size) in enumerate(
            (
                (q_turn, q_all.at[c, h], q_width),
                (k_turn, k_mine.at[h], width),
                (v_turn, v_mine.at[h], width),
            )
        )
    ]
    for copy in own_turn:
        copy.start()

    barrier = pltpu.get_barrier_semaphore()
    for e in range(1, n):
        pl.semaphore_signal(
            barrier, inc=1, device_id={"ctx": lax.rem(c + e, n)}, device_id_type=MESH
        )
    for e in range(1, heads):
        pl.semaphore_signal(
            barrier, inc=1, device_id={"head": lax.rem(h + e, heads)}, device_id_type=MESH
        )
    pl.semaphore_wait(barrier, n - 1 + heads - 1)

    swaps = []
    for e in range(1, heads):
        peer = lax.rem(h + e, heads)
        for i, (src, dst, size) in enumerate(
            (
                (q_turn, q_all.at[c, h], q_width),
                (k_turn, k_mine.at[h], width),
                (v_turn, v_mine.at[h], width),
            )
        ):
            swaps.append(
                remote(
                    src.at[:, pl.ds(pl.multiple_of(peer * size, size), size)],
                    dst,
                    swap_send.at[i, e - 1],
                    swap_recv.at[i, e - 1],
                    head=peer,
                )
            )
    for copy in swaps:
        copy.start()
    map_copies = [
        remote(page_map, maps.at[c], map_send.at[e - 1], map_recv.at[e - 1], ctx=lax.rem(c + e, n))
        for e in range(1, n)
    ]
    for copy in map_copies:
        copy.start()
    own_map = pltpu.make_async_copy(page_map, maps.at[c], local_sem.at[5])
    own_map.start()
    for copy in own_turn:
        copy.wait()
    for copy in swaps:
        copy.wait()

    far_q = [
        remote(q_all.at[c], q_all.at[c], far_q_send.at[d - 1], far_q_recv.at[d - 1], ctx=same_core(d))
        for d in range(1, chips)
    ]
    for copy in far_q:
        copy.start()
    near_q = [
        remote(q_all.at[c], q_all.at[c], near_q_send.at[0], near_q_recv.at[0], ctx=sibling)
    ]
    near_q[0].start()

    for copy in pages_in:
        copy.wait()

    def scale_page(j, carry):
        slot = order[j]
        for raw, sent, scale in ((raw_k, sent_k, k_scale), (raw_v, sent_v, v_scale)):
            page = raw[slot]
            for g in range(kv_heads):
                columns = slice(g * head_dim, (g + 1) * head_dim)
                sent[j, :, columns] = (
                    page[:, columns].astype(jnp.float32) * scale[slot, g]
                ).astype(jnp.bfloat16)
        return carry

    lax.fori_loop(0, slots, scale_page, 0)

    for d in range(1, chips):
        far_q[d - 1].wait()
        source = lax.rem(chip + chips - d, chips) * 2 + core
        near_q.append(
            remote(
                q_all.at[source],
                q_all.at[source],
                near_q_send.at[d],
                near_q_recv.at[d],
                ctx=sibling,
            )
        )
        near_q[d].start()

    page_copies = []
    for e in range(1, n):
        peer = lax.rem(c + e, n)
        for i, (sent, recv) in enumerate(((sent_k, recv_k), (sent_v, recv_v))):
            page_copies.append(
                remote(
                    sent.at[pl.ds(peer * per_peer, per_peer)],
                    recv.at[c],
                    page_send.at[i, e - 1],
                    page_recv.at[i, e - 1],
                    ctx=peer,
                )
            )
    for copy in page_copies:
        copy.start()
    own_pages = [
        pltpu.make_async_copy(
            sent.at[pl.ds(c * per_peer, per_peer)], recv.at[c], local_sem.at[6 + i]
        )
        for i, (sent, recv) in enumerate(((sent_k, recv_k), (sent_v, recv_v)))
    ]
    for copy in own_pages:
        copy.start()

    at_once = max(1, min(per_group, 256 // rows))
    chunks = per_group // at_once
    lanes = lax.broadcasted_iota(jnp.int32, (rows, 128), 1)

    def flat(block):
        if part_rows % 16 == 0:
            return block.reshape(rows, block.shape[2])
        wide = block.astype(jnp.float32)
        return jnp.concatenate([wide[i] for i in range(heads)], axis=0).astype(jnp.bfloat16)

    def attend(block, g, chunk):
        first = g * per_group + chunk * at_once
        start = pl.multiple_of(first * head_dim, head_dim)
        own = pl.ds(pl.multiple_of(g * head_dim, head_dim), head_dim)
        q_block = flat(q_all[block, :, :, pl.ds(start, at_once * head_dim)])
        query = jnp.concatenate(
            [q_block[:, i * head_dim : (i + 1) * head_dim] for i in range(at_once)], axis=0
        )
        keys = sent_k[:, :, own].reshape(slots * page_rows, head_dim)
        values = sent_v[:, :, own].reshape(slots * page_rows, head_dim)
        turn_keys = flat(k_mine[:, :, own])
        turn_values = flat(v_mine[:, :, own])
        cached = lax.dot_general(query, keys, NT, preferred_element_type=jnp.float32) * factor
        recent = lax.dot_general(query, turn_keys, NT, preferred_element_type=jnp.float32) * factor
        line = lax.broadcasted_iota(jnp.int32, (at_once, rows, rows), 1).reshape(
            at_once * rows, rows
        )
        column = lax.broadcasted_iota(jnp.int32, (at_once * rows, rows), 1)
        visible = c * rows + column <= block * rows + line
        recent = jnp.where(visible, recent, -jnp.inf)
        peak = jnp.maximum(
            jnp.max(cached, axis=1, keepdims=True), jnp.max(recent, axis=1, keepdims=True)
        )
        cached = jnp.exp(cached - peak)
        recent = jnp.exp(recent - peak)
        total = jnp.sum(cached, axis=1, keepdims=True) + jnp.sum(recent, axis=1, keepdims=True)
        mixed = jnp.dot(
            cached.astype(jnp.bfloat16), values, preferred_element_type=jnp.float32
        ) + jnp.dot(recent.astype(jnp.bfloat16), turn_values, preferred_element_type=jnp.float32)
        kept = stats[block]
        for i in range(at_once):
            these = slice(i * rows, (i + 1) * rows)
            acc[block, :, pl.ds(pl.multiple_of(start + i * head_dim, head_dim), head_dim)] = mixed[
                these
            ]
            kept = jnp.where(lanes == first + i, peak[these], kept)
            kept = jnp.where(lanes == q_heads + first + i, total[these], kept)
        stats[block] = kept

    def attend_block(block):
        stats[block] = jnp.zeros((rows, 128), jnp.float32)

        def step(i, carry):
            attend(block, i // chunks, i % chunks)
            return carry

        lax.fori_loop(0, kv_heads * chunks, step, 0)

    near = []

    def give(d):
        block = other_core(d)
        for i, (src, dst) in enumerate(((acc, sib_acc), (stats, sib_stats))):
            copy = remote(
                src.at[block], dst.at[d], near_send.at[i, d], near_recv.at[i, d], ctx=sibling
            )
            copy.start()
            near.append(copy)

    attend_block(c)
    near_q[0].wait()
    attend_block(sibling)
    give(0)
    for d in range(1, chips):
        near_q[d].wait()

    def far_other(d, carry):
        attend_block(other_core(d))
        return carry

    def far_same(d, carry):
        attend_block(same_core(d))
        return carry

    lax.fori_loop(1, chips, far_other, 0)
    for d in range(1, chips):
        give(d)
    lax.fori_loop(1, chips, far_same, 0)

    def pick(stat, i):
        return stat[:, i : i + 1], stat[:, q_heads + i : q_heads + i + 1]

    def join(stats_a, read_a, stats_b, read_b, write):
        kept = jnp.zeros((rows, 128), jnp.float32)
        for i in range(q_heads):
            columns = slice(i * head_dim, (i + 1) * head_dim)
            peak_a, total_a = pick(stats_a, i)
            peak_b, total_b = pick(stats_b, i)
            peak = jnp.maximum(peak_a, peak_b)
            weight_a = jnp.exp(peak_a - peak)
            weight_b = jnp.exp(peak_b - peak)
            total = total_a * weight_a + total_b * weight_b
            mixed = read_a(columns) * weight_a + read_b(columns).astype(jnp.float32) * weight_b
            write(columns, mixed, total)
            kept = jnp.where(lanes == i, peak, kept)
            kept = jnp.where(lanes == q_heads + i, total, kept)
        return kept

    far = []
    for d in [*range(1, chips), 0]:
        near[2 * d].wait()
        near[2 * d + 1].wait()
        block = same_core(d)

        def write(columns, mixed, total, d=d):
            if d:
                far_out[d - 1, :, columns] = mixed.astype(jnp.bfloat16)
            elif chips == 1:
                out[:, columns] = (mixed / total).astype(jnp.bfloat16)
            else:
                acc[c, :, columns] = mixed

        kept = join(
            stats[block],
            lambda columns, block=block: acc[block, :, columns],
            sib_stats[d],
            lambda columns, d=d: sib_acc[d, :, columns],
            write,
        )
        if d:
            far_out_stats[d - 1] = kept
            for i, (src, dst) in enumerate(((far_out, far_in), (far_out_stats, far_in_stats))):
                copy = remote(
                    src.at[d - 1],
                    dst.at[d - 1],
                    far_send.at[i, d - 1],
                    far_recv.at[i, d - 1],
                    ctx=block,
                )
                copy.start()
                far.append(copy)
        else:
            stats[c] = kept

    for d in range(1, chips):
        far[2 * (d - 1)].wait()
        far[2 * (d - 1) + 1].wait()
        last = d == chips - 1

        def write_far(columns, mixed, total, last=last):
            if last:
                out[:, columns] = (mixed / total).astype(jnp.bfloat16)
            else:
                acc[c, :, columns] = mixed

        kept = join(
            stats[c],
            lambda columns: acc[c, :, columns],
            far_in_stats[d - 1],
            lambda columns, d=d: far_in[d - 1, :, columns],
            write_far,
        )
        if not last:
            stats[c] = kept

    own_map.wait()
    for copy in own_pages + map_copies + page_copies:
        copy.wait()


def place_kernel(n, maps, attn, recv_k, recv_v, out, out_k, out_v, sem):
    c = lax.axis_index("ctx")
    slots = out_k.shape[0]
    half = slots // 2
    passed = pltpu.make_async_copy(attn, out, sem.at[2])
    passed.start()
    for source in range(n):

        def visit(s, count, source=source):
            page = maps[source, 0, s]
            block = page // half
            within = page % half
            first = block == c
            mine = first | (block == 2 * n - 1 - c)

            @pl.when(mine)
            def _():
                place = jnp.where(first, within, half + within)
                for recv, to, i in ((recv_k, out_k, 0), (recv_v, out_v, 1)):
                    pltpu.make_async_copy(recv.at[source, count], to.at[place], sem.at[i]).start()

            return count + mine.astype(jnp.int32)

        lax.fori_loop(0, slots, visit, jnp.int32(0))
    passed.wait()
    for to, i in ((out_k, 0), (out_v, 1)):
        pltpu.make_async_copy(to, to, sem.at[i]).wait()


def local(q_turn, k_turn, v_turn, cache_k, cache_v, k_scale, v_scale, page_map):
    n = lax.axis_size("ctx")
    heads = lax.axis_size("head")
    slots, page_rows, width = cache_k.shape
    kv_heads = k_scale.shape[1]
    head_dim = width // kv_heads
    part_rows = q_turn.shape[0]
    rows = part_rows * heads
    q_width = q_turn.shape[1] // heads
    half = slots // 2
    per_peer = slots // n
    chips = n // 2
    bf16, f32 = jnp.bfloat16, jnp.float32

    block = page_map // half
    owner = jnp.where(block < n, block, 2 * n - 1 - block)
    slot = jnp.arange(slots, dtype=jnp.int32)
    before = (owner[None, :] == owner[:, None]) & (slot[None, :] < slot[:, None])
    rank = owner * per_peer + jnp.sum(before, axis=1, dtype=jnp.int32)
    order = jnp.sum(
        jnp.where(rank[None, :] == slot[:, None], slot[None, :], 0), axis=1, dtype=jnp.int32
    )
    map_row = jnp.pad(page_map, (0, -slots % 128))[None, :]

    smem = pl.BlockSpec(memory_space=pltpu.SMEM)
    vmem = pl.BlockSpec(memory_space=pltpu.VMEM)
    anywhere = pl.BlockSpec(memory_space=pl.ANY)
    dma = pltpu.SemaphoreType.DMA
    received = jax.ShapeDtypeStruct((n, per_peer, page_rows, width), bf16)
    some = max(1, chips - 1)
    keys = slots * page_rows + rows
    attn, recv_k, recv_v, maps = pl.pallas_call(
        functools.partial(main_kernel, n, heads, head_dim),
        out_shape=(
            jax.ShapeDtypeStruct((rows, q_width), bf16),
            received,
            received,
            jax.ShapeDtypeStruct((n, *map_row.shape), jnp.int32),
        ),
        in_specs=[smem] * 3 + [vmem] + [anywhere] * 5,
        out_specs=(vmem, anywhere, anywhere, vmem),
        scratch_shapes=[
            pltpu.VMEM((slots, page_rows, width), bf16),
            pltpu.VMEM((slots, page_rows, width), bf16),
            pltpu.VMEM((slots, page_rows, width), bf16),
            pltpu.VMEM((slots, page_rows, width), bf16),
            pltpu.VMEM((n, heads, part_rows, q_width), bf16),
            pltpu.VMEM((heads, part_rows, width), bf16),
            pltpu.VMEM((heads, part_rows, width), bf16),
            pltpu.VMEM((n, rows, q_width), f32),
            pltpu.VMEM((n, rows, 128), f32),
            pltpu.VMEM((chips, rows, q_width), f32),
            pltpu.VMEM((chips, rows, 128), f32),
            pltpu.VMEM((some, rows, q_width), bf16),
            pltpu.VMEM((some, rows, 128), f32),
            pltpu.VMEM((some, rows, q_width), bf16),
            pltpu.VMEM((some, rows, 128), f32),
            dma((8,)),
            dma((3, max(1, heads - 1))),
            dma((3, max(1, heads - 1))),
            dma((some,)),
            dma((some,)),
            dma((chips,)),
            dma((chips,)),
            dma((2, n - 1)),
            dma((2, n - 1)),
            dma((n - 1,)),
            dma((n - 1,)),
            dma((2, chips)),
            dma((2, chips)),
            dma((2, some)),
            dma((2, some)),
        ],
        compiler_params=pltpu.CompilerParams(
            collective_id=0, has_side_effects=True, vmem_limit_bytes=48 * 2**20
        ),
        cost_estimate=pl.CostEstimate(
            flops=4 * n * rows * q_width * keys,
            bytes_accessed=8 * slots * page_rows * width * 2,
            transcendentals=n * rows * (q_width // head_dim) * keys,
        ),
        name="exchange_and_attend",
    )(order, k_scale, v_scale, map_row, q_turn, k_turn, v_turn, cache_k, cache_v)

    paged = jax.ShapeDtypeStruct((slots, page_rows, width), bf16)
    attn_out, paired_k, paired_v = pl.pallas_call(
        functools.partial(place_kernel, n),
        out_shape=(jax.ShapeDtypeStruct((rows, q_width), bf16), paged, paged),
        in_specs=[smem, anywhere, anywhere, anywhere],
        out_specs=(anywhere, anywhere, anywhere),
        scratch_shapes=[dma((3,))],
        cost_estimate=pl.CostEstimate(
            flops=0, bytes_accessed=4 * slots * page_rows * width * 2, transcendentals=0
        ),
        name="place_pages",
    )(maps, attn, recv_k, recv_v)
    flat = (slots * page_rows, width)
    return (attn_out, paired_k.reshape(flat), paired_v.reshape(flat))


def solution(mesh):
    return jax.shard_map(
        local,
        mesh=mesh,
        in_specs=(
            P(("rep", "ctx", "head"), None),
            P(("rep", "ctx", "head"), None),
            P(("rep", "ctx", "head"), None),
            P(("rep", "ctx"), None, "head"),
            P(("rep", "ctx"), None, "head"),
            P(("rep", "ctx"), "head"),
            P(("rep", "ctx"), "head"),
            P(("rep", "ctx")),
        ),
        out_specs=(P(("rep", "ctx"), "head"), P(("rep", "ctx"), "head"), P(("rep", "ctx"), "head")),
        check_vma=False,
    )
```

time: 552 us -> 242 us (0.44)
  Pallas kernels: 0 us -> 230 us
  matrix products: 161 us -> 0 us
  waiting for transfers between devices: 112 us -> 0 us
  loops' own time: 83.7 us -> 0 us
  local copies, waits for them, and re-layouts: 87.9 us -> 8.91 us
  other arithmetic: 41.8 us -> 1.63 us
  blocking collectives: 30.3 us -> 0 us
  starting transfers between devices: 15.1 us -> 0 us
  between operations: 15.1 us -> 0.66 us
    pallas_call x0 -> x2, Pallas kernels: none -> 230 us  [the longest x1 145 us: local(): pl.pallas_call(functools.partial(place_kernel, n), out_shape=(jax.ShapeDt...]
    dot_general x128 -> x0, matrix products: 161 us -> none  [the longest x32 70.2 us: one_head(): jnp.dot(cached_e.astype(jnp.bfloat16), cv, preferred_element_type=jnp.flo...]
    all_to_all x4 -> x0, waiting for transfers between devices: 89.8 us -> none  [the longest x1 46.5 us: local(): lax.all_to_all(send_k, 'ctx', split_axis=0, concat_axis=0, tiled=True)]
    another operation x2 -> x0, loops' own time: 83.7 us -> none  [the longest x1 83.6 us: attend(): lax.map(one_head, (by_head, jnp.arange(q_heads, dtype=jnp.int32)))]
    dynamic_slice x36 -> x0, local copies, waits for them, and re-layouts: 27.6 us -> none  [the longest x32 19.7 us: attend(): lax.map(one_head, (by_head, jnp.arange(q_heads, dtype=jnp.int32)))]
    all_gather x2 -> x0, waiting for transfers between devices: 21.8 us -> none  [the longest x1 21.8 us: joined(): pieces = jax.tree.map(lambda part: lax.all_gather(part, axis), value)]
    add x40 -> x1, other arithmetic: 18.6 us -> 0.67 us  [local(): rank = owner * per_peer + jnp.sum(before, axis=1, dtype=jnp.int32)]
    all_to_all x4 -> x0, starting transfers between devices: 15 us -> none  [the longest x1 4.79 us: local(): lax.all_to_all(send_k, 'ctx', split_axis=0, concat_axis=0, tiled=True)]
  transfers between devices with their start and end apart: 6 -> 0, of which waited for: 4 -> 0; matrix products, arithmetic and copies ran while one was open for 6% -> 0% of each run, Pallas kernels for 0% -> 0%
where the time goes in v1:
time: 242 us
  Pallas kernels  230 us (95%)
  local copies, waits for them, and re-layouts  8.91 us (4%)
    pallas_call x1, Pallas kernels, local(): pl.pallas_call(functools.partial(place_kernel, n), out_shape=(jax.ShapeDt...  145 us
    pallas_call x1, Pallas kernels, local(): pl.pallas_call(functools.partial(main_kernel, n, heads, head_dim), out_sh...  85.7 us
    unnamed x16, local copies, waits for them, and re-layouts  8.25 us

profile of v1, /device:TPU:0, one launch (start us, length us, event | category | flops | bytes accessed | tf_op | source)
XLA Modules:
  0.0 241.6 jit_solution(4779335163733542788)
XLA Ops:
  0.6 0.7 pad_bitcast_fusion.page_map
  1.3 0.7 compare_select_fusion
  2.0 0.2 convert_reduce_fusion
  2.1 0.7 multiply_add_fusion
  2.8 0.1 select_reduce_fusion.order
  2.9 0.8 copy.13.k_scale
  3.7 0.8 copy.14.v_scale
  4.5 0.0 copy-start.4
  4.5 1.0 copy-done.4
  5.5 0.0 copy-start.5
  5.5 0.8 copy-done.5
  6.3 0.0 copy-start.6
  6.3 0.8 copy-done.6
  7.2 85.7 %exchange_and_attend.1 = (bf16[64,4096]{1,0:T(8,128)(2,1)S(1)}, bf16[4,8,64,512]{3,2,1,0:T(8,128)(2,1)S(1)}, bf16[4,8,64,512]{3,2,1,0:T(8,128)(2,1)S(1)}, s32[4,1,128]{2,1,0:T(1,128)S(1)}) custom-call(s32[32]{0:T(128)S(1)} %select_reduce_fusion.order, f32[32,4]{1,0:T(8,128)S(1)} %copy.13.k_scale, f32[32,4]{1,0:T(8,128)S(1)} %copy.14.v_scale, ...), custom_call_target="tpu_custom_call" | custom-call | flops 8858370048 | bytes 16777216 | tf_op jit(solution)/shard_map/exchange_and_attend/pallas_call | solution.py:454
  92.8 0.0 copy-start
  92.9 1.3 copy-done
  94.2 0.0 copy-start.1
  94.2 1.3 copy-done.1
  95.5 0.0 copy-start.2
  95.5 0.8 copy-done.2
  96.3 0.0 copy-start.3
  96.3 0.6 copy-done.3
  96.9 144.8 %place_pages.1 = (bf16[64,4096]{1,0:T(8,128)(2,1)}, bf16[32,64,512]{2,1,0:T(8,128)(2,1)}, bf16[32,64,512]{2,1,0:T(8,128)(2,1)}) custom-call(s32[4,1,128]{2,1,0:T(1,128)} %copy-done.3, bf16[64,4096]{1,0:T(8,128)(2,1)} %copy-done.2, bf16[4,8,64,512]{3,2,1,0:T(8,128)(2,1)} %copy-done, bf16[4,8,64,512]{3,2,1,0:T(8,128)(2,1)} %copy-done.1), custom_call_target="tpu_custom_call" | custom-call | bytes 8388608 | tf_op jit(solution)/shard_map/place_pages/pallas_call | solution.py:508
Async XLA Ops:
  4.5 1.0 copy-start.4
  5.5 0.8 copy-start.5
  6.3 0.8 copy-start.6
  92.8 1.3 copy-start
  94.2 1.3 copy-start.1
  95.5 0.8 copy-start.2
  96.3 0.6 copy-start.3

commit v2 on v1

--- a/solution.py
+++ b/solution.py
@@ -72,7 +72,7 @@
     kv_heads = width // head_dim
     q_heads = q_width // head_dim
     per_group = q_heads // kv_heads
-    factor = 1.0 / math.sqrt(head_dim)
+    factor = math.log2(math.e) / math.sqrt(head_dim)
 
     def remote(src, dst, send, recv, **where):
         return pltpu.make_async_remote_copy(
@@ -177,25 +177,11 @@
             for g in range(kv_heads):
                 columns = slice(g * head_dim, (g + 1) * head_dim)
                 sent[j, :, columns] = (
-                    page[:, columns].astype(jnp.float32) * scale[slot, g]
+                    page[:, columns].astype(jnp.float32) * scale[g, slot]
                 ).astype(jnp.bfloat16)
         return carry
 
     lax.fori_loop(0, slots, scale_page, 0)
-
-    for d in range(1, chips):
-        far_q[d - 1].wait()
-        source = lax.rem(chip + chips - d, chips) * 2 + core
-        near_q.append(
-            remote(
-                q_all.at[source],
-                q_all.at[source],
-                near_q_send.at[d],
-                near_q_recv.at[d],
-                ctx=sibling,
-            )
-        )
-        near_q[d].start()
 
     page_copies = []
     for e in range(1, n):
@@ -243,8 +229,8 @@
         values = sent_v[:, :, own].reshape(slots * page_rows, head_dim)
         turn_keys = flat(k_mine[:, :, own])
         turn_values = flat(v_mine[:, :, own])
-        cached = lax.dot_general(query, keys, NT, preferred_element_type=jnp.float32) * factor
-        recent = lax.dot_general(query, turn_keys, NT, preferred_element_type=jnp.float32) * factor
+        cached = lax.dot_general(query, keys, NT, preferred_element_type=jnp.float32)
+        recent = lax.dot_general(query, turn_keys, NT, preferred_element_type=jnp.float32)
         line = lax.broadcasted_iota(jnp.int32, (at_once, rows, rows), 1).reshape(
             at_once * rows, rows
         )
@@ -254,12 +240,17 @@
         peak = jnp.maximum(
             jnp.max(cached, axis=1, keepdims=True), jnp.max(recent, axis=1, keepdims=True)
         )
-        cached = jnp.exp(cached - peak)
-        recent = jnp.exp(recent - peak)
-        total = jnp.sum(cached, axis=1, keepdims=True) + jnp.sum(recent, axis=1, keepdims=True)
-        mixed = jnp.dot(
-            cached.astype(jnp.bfloat16), values, preferred_element_type=jnp.float32
-        ) + jnp.dot(recent.astype(jnp.bfloat16), turn_values, preferred_element_type=jnp.float32)
+        peak = peak * factor
+        cached = jnp.exp2(cached * factor - peak).astype(jnp.bfloat16)
+        recent = jnp.exp2(recent * factor - peak).astype(jnp.bfloat16)
+
+        def counted(value):
+            return jnp.concatenate([value, jnp.ones_like(value)], axis=1)
+
+        both = jnp.dot(cached, counted(values), preferred_element_type=jnp.float32) + jnp.dot(
+            recent, counted(turn_values), preferred_element_type=jnp.float32
+        )
+        mixed, total = both[:, :head_dim], both[:, head_dim : head_dim + 1]
         kept = stats[block]
         for i in range(at_once):
             these = slice(i * rows, (i + 1) * rows)
@@ -291,6 +282,19 @@
             near.append(copy)
 
     attend_block(c)
+    for d in range(1, chips):
+        far_q[d - 1].wait()
+        source = lax.rem(chip + chips - d, chips) * 2 + core
+        near_q.append(
+            remote(
+                q_all.at[source],
+                q_all.at[source],
+                near_q_send.at[d],
+                near_q_recv.at[d],
+                ctx=sibling,
+            )
+        )
+        near_q[d].start()
     near_q[0].wait()
     attend_block(sibling)
     give(0)
@@ -320,8 +324,8 @@
             peak_a, total_a = pick(stats_a, i)
             peak_b, total_b = pick(stats_b, i)
             peak = jnp.maximum(peak_a, peak_b)
-            weight_a = jnp.exp(peak_a - peak)
-            weight_b = jnp.exp(peak_b - peak)
+            weight_a = jnp.exp2(peak_a - peak)
+            weight_b = jnp.exp2(peak_b - peak)
             total = total_a * weight_a + total_b * weight_b
             mixed = read_a(columns) * weight_a + read_b(columns).astype(jnp.float32) * weight_b
             write(columns, mixed, total)
@@ -447,6 +451,7 @@
     smem = pl.BlockSpec(memory_space=pltpu.SMEM)
     vmem = pl.BlockSpec(memory_space=pltpu.VMEM)
     anywhere = pl.BlockSpec(memory_space=pl.ANY)
+    hbm = pl.BlockSpec(memory_space=pltpu.HBM)
     dma = pltpu.SemaphoreType.DMA
     received = jax.ShapeDtypeStruct((n, per_peer, page_rows, width), bf16)
     some = max(1, chips - 1)
@@ -459,8 +464,8 @@
             received,
             jax.ShapeDtypeStruct((n, *map_row.shape), jnp.int32),
         ),
-        in_specs=[smem] * 3 + [vmem] + [anywhere] * 5,
-        out_specs=(vmem, anywhere, anywhere, vmem),
+        in_specs=[smem] * 3 + [vmem] + [hbm] * 5,
+        out_specs=(vmem, vmem, vmem, vmem),
         scratch_shapes=[
             pltpu.VMEM((slots, page_rows, width), bf16),
             pltpu.VMEM((slots, page_rows, width), bf16),
@@ -502,15 +507,16 @@
             transcendentals=n * rows * (q_width // head_dim) * keys,
         ),
         name="exchange_and_attend",
-    )(order, k_scale, v_scale, map_row, q_turn, k_turn, v_turn, cache_k, cache_v)
+    )(order, k_scale.T, v_scale.T, map_row, q_turn, k_turn, v_turn, cache_k, cache_v)
 
     paged = jax.ShapeDtypeStruct((slots, page_rows, width), bf16)
     attn_out, paired_k, paired_v = pl.pallas_call(
         functools.partial(place_kernel, n),
         out_shape=(jax.ShapeDtypeStruct((rows, q_width), bf16), paged, paged),
         in_specs=[smem, anywhere, anywhere, anywhere],
-        out_specs=(anywhere, anywhere, anywhere),
+        out_specs=(hbm, hbm, hbm),
         scratch_shapes=[dma((3,))],
+        compiler_params=pltpu.CompilerParams(vmem_limit_bytes=2 * 2**20),
         cost_estimate=pl.CostEstimate(
             flops=0, bytes_accessed=4 * slots * page_rows * width * 2, transcendentals=0
         ),

time: 242 us -> 94.4 us (0.39)
  Pallas kernels: 230 us -> 87 us
  local copies, waits for them, and re-layouts: 8.91 us -> 4.74 us
    pallas_call x1, Pallas kernels: 145 us -> 3.27 us  [local(): pl.pallas_call(functools.partial(place_kernel, n), out_shape=(jax.ShapeDt...]
    unnamed x16 -> x10, local copies, waits for them, and re-layouts: 8.25 us -> 4.08 us
where the time goes in v2:
time: 94.4 us; the launch traced here: 94 us
  Pallas kernels  87 us (92%)
  local copies, waits for them, and re-layouts  4.74 us (5%)
  other arithmetic  1.63 us (2%)
    pallas_call x1, Pallas kernels, local(): pl.pallas_call(functools.partial(main_kernel, n, heads, head_dim), out_sh...  83.7 us
    unnamed x10, local copies, waits for them, and re-layouts  4.08 us
    pallas_call x1, Pallas kernels, local(): pl.pallas_call(functools.partial(place_kernel, n), out_shape=(jax.ShapeDt...  3.27 us

profile of v2, /device:TPU:0, one launch (start us, length us, event | category | flops | bytes accessed | tf_op | source)
XLA Modules:
  0.0 94.0 jit_solution(5993912553359934248)
XLA Ops:
  0.6 0.7 pad_bitcast_fusion.page_map
  1.3 0.7 compare_select_fusion
  2.0 0.2 convert_reduce_fusion
  2.1 0.7 multiply_add_fusion
  2.8 0.1 select_reduce_fusion.order
  2.9 0.0 copy-start
  2.9 1.0 %copy-done = bf16[32,8192]{1,0:T(8,128)(2,1)S(1)} copy-done((bf16[32,8192]{1,0:T(8,128)(2,1)S(1)}, bf16[32,8192]{1,0:T(8,128)(2,1)}, u32[]{:S(2)}) %copy-start) | copy-done | bytes 524312
  4.0 0.0 copy-start.1
  4.0 0.8 copy-done.1
  4.8 0.0 copy-start.2
  4.8 0.8 copy-done.2
  5.7 0.0 copy-start.3
  5.7 0.7 copy-done.3
  6.3 0.0 copy-start.4
  6.3 0.7 copy-done.4
  7.0 83.7 %exchange_and_attend.1 = (bf16[64,4096]{1,0:T(8,128)(2,1)S(1)}, bf16[4,8,64,512]{3,2,1,0:T(8,128)(2,1)S(1)}, bf16[4,8,64,512]{3,2,1,0:T(8,128)(2,1)S(1)}, s32[4,1,128]{2,1,0:T(1,128)S(1)}) custom-call(s32[32]{0:T(128)S(1)} %select_reduce_fusion.order, f32[4,32]{1,0:T(4,128)S(1)} %bitcast.6, f32[4,32]{1,0:T(4,128)S(1)} %bitcast.7, ...), custom_call_target="tpu_custom_call" | custom-call | flops 8858370048 | bytes 16777216 | tf_op jit(solution)/shard_map/exchange_and_attend/pallas_call | solution.py:459
  90.7 3.3 %place_pages.1 = (bf16[64,4096]{1,0:T(8,128)(2,1)}, bf16[32,64,512]{2,1,0:T(8,128)(2,1)}, bf16[32,64,512]{2,1,0:T(8,128)(2,1)}) custom-call(s32[4,1,128]{2,1,0:T(1,128)S(1)} %get-tuple-element.10.maps, bf16[64,4096]{1,0:T(8,128)(2,1)S(1)} %get-tuple-element.11.attn, bf16[4,8,64,512]{3,2,1,0:T(8,128)(2,1)S(1)} %get-tuple-element.12.recv_k, ...), custom_call_target="tpu_custom_call" | custom-call | bytes 8388608 | tf_op jit(solution)/shard_map/place_pages/pallas_call | solution.py:513
Async XLA Ops:
  2.9 1.0 %copy-start = (bf16[32,8192]{1,0:T(8,128)(2,1)S(1)}, bf16[32,8192]{1,0:T(8,128)(2,1)}, u32[]{:S(2)}) copy-start(bf16[32,8192]{1,0:T(8,128)(2,1)} %q_turn.1) | copy-start | bytes 1572868
  4.0 0.8 copy-start.1
  4.8 0.8 copy-start.2
  5.7 0.7 copy-start.3
  6.3 0.7 copy-start.4

commit v3 on v2

--- a/solution.py
+++ b/solution.py
@@ -209,6 +209,7 @@
 
     at_once = max(1, min(per_group, 256 // rows))
     chunks = per_group // at_once
+    paired = 2 if kv_heads * chunks % 2 == 0 else 1
     lanes = lax.broadcasted_iota(jnp.int32, (rows, 128), 1)
 
     def flat(block):
@@ -217,7 +218,8 @@
         wide = block.astype(jnp.float32)
         return jnp.concatenate([wide[i] for i in range(heads)], axis=0).astype(jnp.bfloat16)
 
-    def attend(block, g, chunk):
+    def scores(block, i):
+        g, chunk = i // chunks, i % chunks
         first = g * per_group + chunk * at_once
         start = pl.multiple_of(first * head_dim, head_dim)
         own = pl.ds(pl.multiple_of(g * head_dim, head_dim), head_dim)
@@ -226,11 +228,14 @@
             [q_block[:, i * head_dim : (i + 1) * head_dim] for i in range(at_once)], axis=0
         )
         keys = sent_k[:, :, own].reshape(slots * page_rows, head_dim)
-        values = sent_v[:, :, own].reshape(slots * page_rows, head_dim)
         turn_keys = flat(k_mine[:, :, own])
-        turn_values = flat(v_mine[:, :, own])
         cached = lax.dot_general(query, keys, NT, preferred_element_type=jnp.float32)
         recent = lax.dot_general(query, turn_keys, NT, preferred_element_type=jnp.float32)
+        return first, start, own, cached, recent
+
+    def finish(block, first, start, own, cached, recent):
+        values = sent_v[:, :, own].reshape(slots * page_rows, head_dim)
+        turn_values = flat(v_mine[:, :, own])
         line = lax.broadcasted_iota(jnp.int32, (at_once, rows, rows), 1).reshape(
             at_once * rows, rows
         )
@@ -265,21 +270,24 @@
         stats[block] = jnp.zeros((rows, 128), jnp.float32)
 
         def step(i, carry):
-            attend(block, i // chunks, i % chunks)
+            ready = [scores(block, i * paired + k) for k in range(paired)]
+            for one in ready:
+                finish(block, *one)
             return carry
 
-        lax.fori_loop(0, kv_heads * chunks, step, 0)
-
-    near = []
+        lax.fori_loop(0, kv_heads * chunks // paired, step, 0)
+
+    near = {}
 
     def give(d):
         block = other_core(d)
+        near[d] = []
         for i, (src, dst) in enumerate(((acc, sib_acc), (stats, sib_stats))):
             copy = remote(
                 src.at[block], dst.at[d], near_send.at[i, d], near_recv.at[i, d], ctx=sibling
             )
             copy.start()
-            near.append(copy)
+            near[d].append(copy)
 
     attend_block(c)
     for d in range(1, chips):
@@ -295,9 +303,6 @@
             )
         )
         near_q[d].start()
-    near_q[0].wait()
-    attend_block(sibling)
-    give(0)
     for d in range(1, chips):
         near_q[d].wait()
 
@@ -335,8 +340,12 @@
 
     far = []
     for d in [*range(1, chips), 0]:
-        near[2 * d].wait()
-        near[2 * d + 1].wait()
+        if d == 0:
+            near_q[0].wait()
+            attend_block(sibling)
+            give(0)
+        for copy in near[d]:
+            copy.wait()
         block = same_core(d)
 
         def write(columns, mixed, total, d=d):

time: 94.4 us -> 94.3 us (level)
  no operation moved by 1% of the time
where the time goes in v3:
time: 94.3 us; the launch traced here: 93.9 us
  Pallas kernels  86.9 us (92%)
  local copies, waits for them, and re-layouts  4.74 us (5%)
  other arithmetic  1.63 us (2%)
    pallas_call x1, Pallas kernels, local(): pl.pallas_call(functools.partial(main_kernel, n, heads, head_dim), out_sh...  83.7 us
    unnamed x10, local copies, waits for them, and re-layouts  4.08 us
    pallas_call x1, Pallas kernels, local(): pl.pallas_call(functools.partial(place_kernel, n), out_shape=(jax.ShapeDt...  3.17 us

profile of v3, /device:TPU:0, one launch (start us, length us, event | category | flops | bytes accessed | tf_op | source)
XLA Modules:
  0.0 93.9 jit_solution(3288928552845024267)
XLA Ops:
  0.6 0.7 pad_bitcast_fusion.page_map
  1.3 0.7 compare_select_fusion
  2.0 0.2 convert_reduce_fusion
  2.1 0.7 multiply_add_fusion
  2.8 0.1 select_reduce_fusion.order
  2.9 0.0 copy-start
  2.9 1.0 %copy-done = bf16[32,8192]{1,0:T(8,128)(2,1)S(1)} copy-done((bf16[32,8192]{1,0:T(8,128)(2,1)S(1)}, bf16[32,8192]{1,0:T(8,128)(2,1)}, u32[]{:S(2)}) %copy-start) | copy-done | bytes 524312
  4.0 0.0 copy-start.1
  4.0 0.8 copy-done.1
  4.8 0.0 copy-start.2
  4.8 0.8 copy-done.2
  5.7 0.0 copy-start.3
  5.7 0.7 copy-done.3
  6.3 0.0 copy-start.4
  6.3 0.7 copy-done.4
  7.0 83.7 %exchange_and_attend.1 = (bf16[64,4096]{1,0:T(8,128)(2,1)S(1)}, bf16[4,8,64,512]{3,2,1,0:T(8,128)(2,1)S(1)}, bf16[4,8,64,512]{3,2,1,0:T(8,128)(2,1)S(1)}, s32[4,1,128]{2,1,0:T(1,128)S(1)}) custom-call(s32[32]{0:T(128)S(1)} %select_reduce_fusion.order, f32[4,32]{1,0:T(4,128)S(1)} %bitcast.6, f32[4,32]{1,0:T(4,128)S(1)} %bitcast.7, ...), custom_call_target="tpu_custom_call" | custom-call | flops 8858370048 | bytes 16777216 | tf_op jit(solution)/shard_map/exchange_and_attend/pallas_call | solution.py:468
  90.7 3.2 %place_pages.1 = (bf16[64,4096]{1,0:T(8,128)(2,1)}, bf16[32,64,512]{2,1,0:T(8,128)(2,1)}, bf16[32,64,512]{2,1,0:T(8,128)(2,1)}) custom-call(s32[4,1,128]{2,1,0:T(1,128)S(1)} %get-tuple-element.10.maps, bf16[64,4096]{1,0:T(8,128)(2,1)S(1)} %get-tuple-element.11.attn, bf16[4,8,64,512]{3,2,1,0:T(8,128)(2,1)S(1)} %get-tuple-element.12.recv_k, ...), custom_call_target="tpu_custom_call" | custom-call | bytes 8388608 | tf_op jit(solution)/shard_map/place_pages/pallas_call | solution.py:522
Async XLA Ops:
  2.9 1.0 %copy-start = (bf16[32,8192]{1,0:T(8,128)(2,1)S(1)}, bf16[32,8192]{1,0:T(8,128)(2,1)}, u32[]{:S(2)}) copy-start(bf16[32,8192]{1,0:T(8,128)(2,1)} %q_turn.1) | copy-start | bytes 1572868
  4.0 0.8 copy-start.1
  4.8 0.8 copy-start.2
  5.7 0.7 copy-start.3
  6.3 0.7 copy-start.4
